TPU v7x, 128 devices: a whole 4x4x4 slice. The times are simulated.
128 devices in a mesh: mem: 32 (over x, z, core), feat: 4 (over y).
Axes of the slice: x: 4, y: 4, z: 4, core: 2. Of those that a mesh axis runs over, the one named last changes fastest.
Arguments:
- events: bfloat16 [8192, 32, 256], P('mem'), may hold values from -6 to 6
- w_in: bfloat16 [256, 1024], P(None, 'feat'), may hold values from -0.375 to 0.375
- w_out: bfloat16 [1024, 256], P('feat'), may hold values from -0.1875 to 0.1875
- probe_vectors: bfloat16 [8192, 256], P(('mem', 'feat')), may hold values from -8 to 8
- key_queue: bfloat16 [262144, 256], P('mem'), may hold values from -1 to 1
- target_position: int32 [8192], P(('mem', 'feat')), may hold values from 0 to 262143
- pointer: int32 [1], replicated, may hold values from 0 to 262143
Outputs:
- loss: float32 [8192], P(('mem', 'feat'))
- probe_derivative: float32 [8192, 256], P(('mem', 'feat'))
- new_memory: bfloat16 [262144, 256], P('mem')
All inputs are finite; a program needn't handle non-finite values.
Results may differ from a plain program's by a relative error of at most 0.0017.
Values may be sent and summed in bfloat16 or wider, within the bound.
No kernel may reach another device: no remote copies, remote signals or barrier semaphores. Data moves between devices by JAX's collectives and lax.ppermute only.
A program may use at most 64 MiB of HBM per device.

v0:
```python
import jax
import jax.numpy as jnp
from jax import lax
from jax.sharding import PartitionSpec as P

inverse_softness = 14.0
epsilon = 1e-06


def normalize_keys(raw_key):
    scaled = (
        raw_key * lax.rsqrt(jnp.mean(raw_key * raw_key, axis=1, keepdims=True) + epsilon) / 16.0
    )
    return scaled.astype(jnp.bfloat16)


def slot_scores(query_rows, queue_position_span):
    similarity_entry = lax.dot_general(
        query_rows,
        queue_position_span,
        (((1,), (1,)), ((), ())),
        preferred_element_type=jnp.float32,
    )
    return similarity_entry * inverse_softness


def shards(events, w_in, w_out, probe_vectors, key_queue, target_position, pointer):
    sessions = events.shape[0]
    flattened = events.reshape(sessions * events.shape[1], events.shape[2])
    activation = jax.nn.gelu(jnp.dot(flattened, w_in, preferred_element_type=jnp.float32))
    pooled = jnp.mean(
        activation.reshape(sessions, events.shape[1], activation.shape[1]), axis=1
    ).astype(jnp.bfloat16)
    partial_key = jnp.dot(pooled, w_out, preferred_element_type=jnp.float32)
    key_whole = lax.psum(partial_key, "feat")
    keys_all = lax.all_gather(normalize_keys(key_whole), "mem", axis=0, tiled=True)
    cycle_size = key_queue.shape[0]
    slots_total = cycle_size * lax.axis_size("mem")
    cycle_first = lax.axis_index("mem") * cycle_size
    global_slot = cycle_first + jnp.arange(cycle_size, dtype=jnp.int32)
    offsets = (global_slot - pointer[0]) % slots_total
    session_count = keys_all.shape[0]
    picked = jnp.take(keys_all, jnp.minimum(offsets, session_count - 1), axis=0)
    new_memory = jnp.where((offsets < session_count)[:, None], picked, key_queue)
    gathered_queries, gathered_positive = (
        lax.all_gather(probe_vectors, "mem", axis=0, tiled=True),
        lax.all_gather(target_position, "mem", axis=0, tiled=True),
    )
    row_total = gathered_queries.shape[0]
    block_size = min(1024, cycle_size)
    block_count = cycle_size // block_size
    slot_blocks = key_queue.reshape(block_count, block_size, key_queue.shape[1])
    block_starts = jnp.arange(block_count, dtype=jnp.int32) * block_size
    positions = jnp.arange(block_size, dtype=jnp.int32)
    local_positive = gathered_positive - cycle_first

    def first_pass(carry, item):
        running_max, running_sum, positive_score = carry
        queue_position_span, first_slot = item
        similarity_table = slot_scores(gathered_queries, queue_position_span)
        new_max = jnp.maximum(running_max, jnp.max(similarity_table, axis=1))
        running_sum = running_sum * jnp.exp(running_max - new_max) + jnp.sum(
            jnp.exp(similarity_table - new_max[:, None]), axis=1
        )
        hit = positions[None, :] == (local_positive - first_slot)[:, None]
        positive_score = positive_score + jnp.sum(jnp.where(hit, similarity_table, 0.0), axis=1)
        return ((new_max, running_sum, positive_score), None)

    start_carry = (
        jnp.full((row_total,), -jnp.inf, jnp.float32),
        jnp.zeros((row_total,), jnp.float32),
        jnp.zeros((row_total,), jnp.float32),
    )
    (local_max, local_sum, local_score), stored = lax.scan(
        first_pass, start_carry, (slot_blocks, block_starts)
    )
    top = lax.pmax(local_max, "mem")
    total, positive_score = lax.psum((local_sum * jnp.exp(local_max - top), local_score), "mem")
    own_rows = probe_vectors.shape[0]
    own_first = lax.axis_index("mem") * own_rows
    loss_all = top + jnp.log(total) - positive_score
    loss = lax.dynamic_slice_in_dim(loss_all, own_first, own_rows)

    def add_weighted(collected_denominator, similarity_table, queue_position_span):
        weights = (jnp.exp(similarity_table - top[:, None]) / total[:, None]).astype(jnp.bfloat16)
        return collected_denominator + jnp.dot(
            weights, queue_position_span, preferred_element_type=jnp.float32
        )

    start_sum = jnp.zeros((row_total, key_queue.shape[1]), jnp.float32)

    def second_pass(collected_denominator, queue_position_span):
        return (
            add_weighted(
                collected_denominator,
                slot_scores(gathered_queries, queue_position_span),
                queue_position_span,
            ),
            None,
        )

    collected_denominator, unused_part = lax.scan(second_pass, start_sum, slot_blocks)
    inside = (local_positive >= 0) & (local_positive < cycle_size)
    paired_entries = jnp.take(
        key_queue, jnp.clip(local_positive, 0, cycle_size - 1), axis=0
    ).astype(jnp.float32)
    paired_entries = jnp.where(inside[:, None], paired_entries, 0.0)
    summed_derivative_terms = lax.psum(
        inverse_softness * (collected_denominator - paired_entries), "mem"
    )
    probe_derivative = lax.dynamic_slice_in_dim(summed_derivative_terms, own_first, own_rows, 0)
    return (loss, probe_derivative, new_memory)


def solution(mesh):
    placed = (
        P("mem", None, None),
        P(None, "feat"),
        P("feat", None),
        P(("mem", "feat"), None),
        P("mem", None),
        P(("mem", "feat")),
        P(),
    )
    return jax.shard_map(
        shards,
        mesh=mesh,
        in_specs=placed,
        out_specs=(P(("mem", "feat")), P(("mem", "feat"), None), P("mem", None)),
        check_vma=False,
    )
```

profile of v0, /device:TPU:1, one launch (start us, length us, event | category | flops | bytes accessed | tf_op | source)
XLA Modules:
  0.0 587.6 jit_solution(14332669593911734869)
XLA Ops:
  8.1 0.7 all-gather.3.cloned.1.call-update
  8.8 0.1 copy-done
  8.9 5.8 bitcast_reduce_fusion
  14.7 0.9 fusion.24
  15.8 0.6 dynamic-slice
  17.0 0.3 dynamic-update-slice
  17.3 15.9 %all-reduce = s32[2048]{0:T(1024)S(1)} all-reduce(s32[2048]{0:T(1024)S(1)} %dynamic-update-slice), channel_id=1, replica_groups=mesh['mem'=32,'feat'=4] {'mem'}, use_global_device_ids=true, to_apply=%add | all-reduce | flops 2048 | bytes 16384
  33.3 9.4 %gather_fusion = bf16[2048,256]{1,0:T(8,128)(2,1)S(1)} fusion(bf16[8192,256]{1,0:T(8,128)(2,1)} %param.15, s32[2048]{0:T(1024)S(1)} %fusion.30), kind=kCustom, calls=%fused_computation | custom fusion | bytes 2105344 | tf_op jit(solution)/shard_map/jit(_take)/gather | solution.py:104
  42.6 15.0 %all-gather.3.cloned.1.call-done = bf16[2048,256]{1,0:T(8,128)(2,1)} async-done(((bf16[64,256]{1,0:T(8,128)(2,1)}), bf16[2048,256]{1,0:T(8,128)(2,1)}) %all-gather.3.cloned.1.call-update) | async-done | bytes 1048592 | tf_op jit(solution)/shard_map/all_gather | solution.py:46
  57.7 95.2 %while.26 = (s32[]{:T(128)}, f32[2048]{0:T(1024)S(1)}, f32[2048]{0:T(1024)S(1)}, f32[2048]{0:T(1024)S(1)}, bf16[8,1024,256]{2,1,0:T(8,128)(2,1)}, /*index=5*/bf1...) while((s32[]{:T(128)}, f32[2048]{0:T(1024)S(1)}, ...), condition=%wide.region_4.5_spmd.clone, body=%wide.region_0.4_spmd.clone.sunk | while | flops 1090533376 | bytes 18514560 | solution.py:74
  57.7 5.9 %multiply_reduce_fusion.3 = (f32[2048]{0:T(1024)S(1)}, f32[1024,2048]{1,0:T(8,128)}) fusion(bf16[2048,256]{1,0:T(8,128)(2,1)} %get-tuple-element.301, bf16[8,1024,256]{2,1,0:T(8,128)(2,1)} %get-tuple-element.300, s32[]{:T(128)} %get-tuple-element.286), kind=kOutput, calls=%fused_computation.9.clone.1 | convolution fusion | flops 1077934080 | bytes 9970176 | tf_op jit(solution)/shard_map/while/body/eval_jaxpr/dot_general | solution.py:18
  63.6 0.6 dynamic_slice.51
  64.2 0.6 broadcast_subtract_fusion.4
  64.8 4.7 fusion.43
  69.6 5.9 %multiply_reduce_fusion.3 = (f32[2048]{0:T(1024)S(1)}, f32[1024,2048]{1,0:T(8,128)}) fusion(bf16[2048,256]{1,0:T(8,128)(2,1)} %get-tuple-element.301, bf16[8,1024,256]{2,1,0:T(8,128)(2,1)} %get-tuple-element.300, s32[]{:T(128)} %get-tuple-element.286), kind=kOutput, calls=%fused_computation.9.clone.1 | convolution fusion | flops 1077934080 | bytes 9970176 | tf_op jit(solution)/shard_map/while/body/eval_jaxpr/dot_general | solution.py:18
  75.5 0.6 dynamic_slice.51
  76.1 0.6 broadcast_subtract_fusion.4
  76.7 4.7 fusion.43
  81.5 5.9 %multiply_reduce_fusion.3 = (f32[2048]{0:T(1024)S(1)}, f32[1024,2048]{1,0:T(8,128)}) fusion(bf16[2048,256]{1,0:T(8,128)(2,1)} %get-tuple-element.301, bf16[8,1024,256]{2,1,0:T(8,128)(2,1)} %get-tuple-element.300, s32[]{:T(128)} %get-tuple-element.286), kind=kOutput, calls=%fused_computation.9.clone.1 | convolution fusion | flops 1077934080 | bytes 9970176 | tf_op jit(solution)/shard_map/while/body/eval_jaxpr/dot_general | solution.py:18
  87.4 0.6 dynamic_slice.51
  88.0 0.6 broadcast_subtract_fusion.4
  88.6 4.7 fusion.43
  93.4 5.9 %multiply_reduce_fusion.3 = (f32[2048]{0:T(1024)S(1)}, f32[1024,2048]{1,0:T(8,128)}) fusion(bf16[2048,256]{1,0:T(8,128)(2,1)} %get-tuple-element.301, bf16[8,1024,256]{2,1,0:T(8,128)(2,1)} %get-tuple-element.300, s32[]{:T(128)} %get-tuple-element.286), kind=kOutput, calls=%fused_computation.9.clone.1 | convolution fusion | flops 1077934080 | bytes 9970176 | tf_op jit(solution)/shard_map/while/body/eval_jaxpr/dot_general | solution.py:18
  99.3 0.6 dynamic_slice.51
  99.9 0.6 broadcast_subtract_fusion.4
  100.5 4.7 fusion.43
  105.3 5.9 %multiply_reduce_fusion.3 = (f32[2048]{0:T(1024)S(1)}, f32[1024,2048]{1,0:T(8,128)}) fusion(bf16[2048,256]{1,0:T(8,128)(2,1)} %get-tuple-element.301, bf16[8,1024,256]{2,1,0:T(8,128)(2,1)} %get-tuple-element.300, s32[]{:T(128)} %get-tuple-element.286), kind=kOutput, calls=%fused_computation.9.clone.1 | convolution fusion | flops 1077934080 | bytes 9970176 | tf_op jit(solution)/shard_map/while/body/eval_jaxpr/dot_general | solution.py:18
  111.2 0.6 dynamic_slice.51
  111.8 0.6 broadcast_subtract_fusion.4
  112.4 4.7 fusion.43
  117.2 5.9 %multiply_reduce_fusion.3 = (f32[2048]{0:T(1024)S(1)}, f32[1024,2048]{1,0:T(8,128)}) fusion(bf16[2048,256]{1,0:T(8,128)(2,1)} %get-tuple-element.301, bf16[8,1024,256]{2,1,0:T(8,128)(2,1)} %get-tuple-element.300, s32[]{:T(128)} %get-tuple-element.286), kind=kOutput, calls=%fused_computation.9.clone.1 | convolution fusion | flops 1077934080 | bytes 9970176 | tf_op jit(solution)/shard_map/while/body/eval_jaxpr/dot_general | solution.py:18
  123.1 0.6 dynamic_slice.51
  123.7 0.6 broadcast_subtract_fusion.4
  124.3 4.7 fusion.43
  129.1 5.9 %multiply_reduce_fusion.3 = (f32[2048]{0:T(1024)S(1)}, f32[1024,2048]{1,0:T(8,128)}) fusion(bf16[2048,256]{1,0:T(8,128)(2,1)} %get-tuple-element.301, bf16[8,1024,256]{2,1,0:T(8,128)(2,1)} %get-tuple-element.300, s32[]{:T(128)} %get-tuple-element.286), kind=kOutput, calls=%fused_computation.9.clone.1 | convolution fusion | flops 1077934080 | bytes 9970176 | tf_op jit(solution)/shard_map/while/body/eval_jaxpr/dot_general | solution.py:18
  135.0 0.6 dynamic_slice.51
  135.6 0.6 broadcast_subtract_fusion.4
  136.2 4.7 fusion.43
  141.0 5.9 %multiply_reduce_fusion.3 = (f32[2048]{0:T(1024)S(1)}, f32[1024,2048]{1,0:T(8,128)}) fusion(bf16[2048,256]{1,0:T(8,128)(2,1)} %get-tuple-element.301, bf16[8,1024,256]{2,1,0:T(8,128)(2,1)} %get-tuple-element.300, s32[]{:T(128)} %get-tuple-element.286), kind=kOutput, calls=%fused_computation.9.clone.1 | convolution fusion | flops 1077934080 | bytes 9970176 | tf_op jit(solution)/shard_map/while/body/eval_jaxpr/dot_general | solution.py:18
  146.9 0.6 dynamic_slice.51
  147.5 0.6 broadcast_subtract_fusion.4
  148.1 4.7 fusion.43
  152.9 63.2 %pmax.7 = f32[2048]{0:T(1024)S(1)} all-reduce(f32[2048]{0:T(1024)S(1)} %get-tuple-element.84), channel_id=1, replica_groups=mesh['mem'=32,'feat'=4] {'mem'}, use_global_device_ids=true, to_apply=%region_5.6 | all-reduce | flops 2048 | bytes 16384 | tf_op jit(solution)/shard_map/pmax | solution.py:77
  216.1 121.4 %all-reduce.1 = (f32[2048]{0:T(1024)S(1)}, f32[2048]{0:T(1024)S(1)}) all-reduce(f32[2048]{0:T(1024)S(1)} %get-tuple-element.86, f32[2048]{0:T(1024)S(1)} %exponential_multiply_fusion), channel_id=1, replica_groups=mesh['mem'=32,'feat'=4] {'mem'}, use_global_device_ids=true, to_apply=%region_7.8 | all-reduce | flops 4096 | bytes 32768 | tf_op jit(solution)/shard_map/psum | solution.py:78
  337.5 40.7 %while.27 = (s32[]{:T(128)}, f32[2048,256]{1,0:T(8,128)S(1)}, bf16[8,1024,256]{2,1,0:T(8,128)(2,1)}, bf16[2048,256]{1,0:T(8,128)(2,1)}, f32[2048]{0:T(1024)S(1)}, /*index=5*/f32[2048]{0:T(1024)S(1)}, s32[]{:T(128)}, s32[]{:T(128)}) while((s32[]{:T(128)}, f32[2048,256]{1,0:T(8,128)S(1)}, bf16[8,1024,256]{2,1,0:T(8,128)(2,1)}, ...), condition=%wide.region_9.10_spmd.clone, body=%wide.region_8.9_spmd.clone.sunk | while | flops 2156920832 | bytes 6308959 | solution.py:102
  337.5 5.0 convolution_add_fusion.2
  342.6 5.0 convolution_add_fusion.2
  347.7 5.1 convolution_add_fusion.2
  352.7 5.1 convolution_add_fusion.2
  357.8 5.1 convolution_add_fusion.2
  362.9 5.0 convolution_add_fusion.2
  368.0 5.2 convolution_add_fusion.2
  373.2 5.1 convolution_add_fusion.2
  378.2 2.7 subtract_multiply_fusion
  381.0 0.0 all-gather.5.cloned.1.call-start
  381.1 1.1 multiply_reduce_fusion.1
  382.2 1.7 multiply_convert_fusion
  384.6 0.2 compare_select_fusion
  384.8 0.6 dynamic-slice_subtract_fusion
  385.4 104.2 %all-reduce.5.cloned.1.call-done = f32[2048,256]{1,0:T(8,128)} async-done(((f32[2048,256]{1,0:T(8,128)}), f32[2048,256]{1,0:T(8,128)}) %all-reduce.5.cloned.1.call-update) | async-done | bytes 2097168 | tf_op jit(solution)/shard_map/psum | solution.py:108
  489.6 1.5 constant_dynamic-slice_fusion
  491.1 47.1 %all-gather.5.cloned.1.call-done = bf16[8192,256]{1,0:T(8,128)(2,1)} async-done(((bf16[256,256]{1,0:T(8,128)(2,1)}), bf16[8192,256]{1,0:T(8,128)(2,1)}) %all-gather.5.cloned.1.call-update) | async-done | bytes 4194320 | tf_op jit(solution)/shard_map/all_gather | solution.py:36
  538.2 33.9 %gather_fusion.1 = bf16[8192,256]{1,0:T(8,128)(2,1)} fusion(bf16[8192,256]{1,0:T(8,128)(2,1)} %all-gather.5.cloned.1.call-done, s32[8192]{0:T(1024)S(1)} %broadcast_clamp_fusion), kind=kCustom, calls=%fused_computation.1 | custom fusion | bytes 8421376 | tf_op jit(solution)/shard_map/jit(_take)/gather | solution.py:43
  572.1 7.9 %select_select_fusion = bf16[8192,256]{1,0:T(8,128)(2,1)} fusion(bf16[8192,256]{1,0:T(8,128)(2,1)} %bitcast.48, bf16[8192,256]{1,0:T(8,128)(2,1)} %gather_fusion.1, pred[8192]{0:T(1024)(128)(4,1)S(1)} %get-tuple-element.176, pred[8192]{0:T(1024)(128)(4,1)S(1)} %get-tuple-element.177), kind=kLoop, calls=%fused_computation.34 | loop fusion | flops 4194304 | bytes 12599296 | tf_op jit(solution)/shard_map/jit(_where)/select_n | solution.py:44
  (51 shorter events, 0.5 us)
Async XLA Ops:
  8.0 0.9 copy-start
  8.0 49.7 %all-gather.3.cloned.1.call-start = ((), (), s32[]{:S(2)}) async-start(), calls=%async_computation | async-start | bytes 1081344 | tf_op jit(solution)/shard_map/all_gather | solution.py:46
  8.7 372.3 %all-reduce.7.cloned.1.call-start = ((), (), s32[]{:S(2)}) async-start(), calls=%async_computation.2 | async-start | bytes 524288 | tf_op jit(solution)/shard_map/psum | solution.py:35
  8.9 5.8 copy-start.1
  8.9 6.8 %copy-start.3 = (u32[128]{0:T(128)S(1)}, u32[128]{0:T(128)}, u32[]{:S(2)}) copy-start(u32[128]{0:T(128)} %constant.115) | copy-start | bytes 1540
  8.9 8.1 %copy-start.2 = (s32[64]{0:T(128)S(1)}, s32[64]{0:T(128)}, u32[]{:S(2)}) copy-start(s32[64]{0:T(128)} %param.16) | copy-start | bytes 772
  15.6 474.0 %all-reduce.5.cloned.1.call-start = ((), (), s32[]{:S(2)}) async-start(), calls=%async_computation.1 | async-start | bytes 4194304 | tf_op jit(solution)/shard_map/psum | solution.py:108
  381.0 157.2 %all-gather.5.cloned.1.call-start = ((), (), s32[]{:S(2)}) async-start(), calls=%async_computation.3 | async-start | bytes 4325376 | tf_op jit(solution)/shard_map/all_gather | solution.py:36
Sparse Core Ops, SparseCore 0:
  11.1 46.5 all-gather.2
Sparse Core Ops, SparseCore 1:
  15.7 42.7 all-reduce.6
  381.1 108.5 all-reduce.4
  492.0 46.1 all-gather.4
where the time goes:
time: 588 us
  blocking collectives  201 us (34%)
  waiting for transfers between devices  167 us (28%)
  matrix products  94.4 us (16%)
  other arithmetic  57.2 us (10%)
  local copies, waits for them, and re-layouts  50.4 us (9%)
  between operations  17.2 us (3%)
    psum x1, blocking collectives, shards(): lax.psum((local_sum * jnp.exp(local_max - top), local_score), 'mem')  121 us
    psum x1, waiting for transfers between devices, shards(): lax.psum(inverse_softness * (collected_denominator - paired_entries), 'mem')  104 us
    pmax x1, blocking collectives, shards(): top = lax.pmax(local_max, 'mem')  63.2 us
    dot_general x8, matrix products, slot_scores(): lax.dot_general(query_rows, queue_position_span, (((1,), (1,)), ((), ()))...  47.2 us
    all_gather x1, waiting for transfers between devices, shards(): lax.all_gather(normalize_keys(key_whole), 'mem', axis=0, tiled=True)  47.1 us
    dot_general x8, matrix products, add_weighted(): jnp.dot(weights, queue_position_span, preferred_element_type=jnp.float32)  40.5 us
    reduce_sum x8, other arithmetic, first_pass(): jnp.sum(jnp.where(hit, similarity_table, 0.0), axis=1)  37.6 us
    gather x1, local copies, waits for them, and re-layouts, shards(): picked = jnp.take(keys_all, jnp.minimum(offsets, session_count - 1), axis=0)  33.9 us
  transfers between devices with their start and end apart: 4, of which 3 were waited for; matrix products, arithmetic and copies ran while one was open for 27% of the time, Pallas kernels for 0%

commit v1 on v0

v1 whole, which is shorter than its diff:
```python
import functools

import jax
import jax.numpy as jnp
from jax import lax
from jax.experimental import pallas as pl
from jax.experimental.pallas import tpu as pltpu
from jax.sharding import Mesh
from jax.sharding import PartitionSpec as P

f32 = jnp.float32
bf16 = jnp.bfloat16
SOFT = 14.0
LOG2E = 1.4426950408889634
LN2 = 0.6931471805599453
C2 = SOFT * LOG2E
EPS = 1e-06
D = 256
EV = 32
OWN = 64
GRP = 256
SLOTS = 8192
SESS = 256
SIZES = (4, 4, 2, 4)
ALL = ("x", "z", "c", "f")
ML = 64
POS = 72
PIECE = 136
BIG = 2.0**90
CONTRACT_LAST = (((1,), (1,)), ((), ()))
VMEM_LIMIT = 50 << 20


def flat(p):
    return ((p[0] * SIZES[1] + p[1]) * SIZES[2] + p[2]) * SIZES[3] + p[3]


def ring(axes, step):
    pairs = []
    for x in range(SIZES[0]):
        for z in range(SIZES[1]):
            for c in range(SIZES[2]):
                for f in range(SIZES[3]):
                    p = [x, z, c, f]
                    k = "xzcf".index(axes[c])
                    p[k] = (p[k] + step) % SIZES[k]
                    pairs.append((flat((x, z, c, f)), flat(p)))
    return pairs


def shift(a, axes, step):
    return lax.ppermute(a, ALL, ring(axes, step % 4))


def swap_cores(a):
    return lax.ppermute(a, "c", [(0, 1), (1, 0)])


def encoder_kernel(ev_ref, w_in_ref, w_out_ref, out_ref, pooled_ref):
    i = pl.program_id(0)
    sessions = ev_ref.shape[0]
    rows = 8
    for s in range(0, sessions, rows):
        x = jnp.dot(
            ev_ref[s : s + rows].reshape(rows * EV, D), w_in_ref[...], preferred_element_type=f32
        )
        inner = x * (0.7978845608028654 + 0.035677408136300125 * (x * x))
        g = x + x * jnp.tanh(inner)
        pooled_ref[pl.ds(i * sessions + s, rows), :] = jnp.sum(
            g.reshape(rows, EV, D), axis=1
        ) * (0.5 / EV)

    @pl.when(i == pl.num_programs(0) - 1)
    def _():
        out_ref[...] = jnp.dot(
            pooled_ref[...].astype(bf16), w_out_ref[...], preferred_element_type=f32
        )


def encode(events, w_in, w_out):
    step = 32
    return pl.pallas_call(
        encoder_kernel,
        grid=(SESS // step,),
        in_specs=[
            pl.BlockSpec((step, EV, D), lambda i: (i, 0, 0)),
            pl.BlockSpec((D, D), lambda i: (0, 0)),
            pl.BlockSpec((D, D), lambda i: (0, 0)),
        ],
        out_specs=pl.BlockSpec((SESS, D), lambda i: (0, 0)),
        out_shape=jax.ShapeDtypeStruct((SESS, D), f32),
        scratch_shapes=[pltpu.VMEM((SESS, D), f32)],
        compiler_params=pltpu.CompilerParams(vmem_limit_bytes=VMEM_LIMIT),
        cost_estimate=pl.CostEstimate(
            flops=2 * SESS * EV * D * D, bytes_accessed=4 << 20, transcendentals=SESS * EV * D
        ),
        name="encoder",
    )(events, w_in, w_out)


def keys_kernel(ptr_ref, a_ref, b_ref, c_ref, d_ref, out_ref):
    raw = (a_ref[...] + b_ref[...]) + (c_ref[...] + d_ref[...])
    scale = lax.rsqrt(jnp.mean(raw * raw, axis=1, keepdims=True) + EPS)
    keys = (raw * scale / 16.0).astype(bf16)
    turn = lax.rem(ptr_ref[0], SESS)
    row = lax.broadcasted_iota(jnp.int32, (SESS, SESS), 0)
    col = lax.broadcasted_iota(jnp.int32, (SESS, SESS), 1)
    source = row - turn
    source = jnp.where(source < 0, source + SESS, source)
    pick = jnp.where(col == source, 1.0, 0.0).astype(bf16)
    out_ref[...] = jnp.dot(pick, keys, preferred_element_type=f32).astype(bf16)


def finish_keys(pointer, parts):
    return pl.pallas_call(
        keys_kernel,
        in_specs=[pl.BlockSpec(memory_space=pltpu.SMEM)]
        + [pl.BlockSpec(memory_space=pltpu.VMEM)] * 4,
        out_specs=pl.BlockSpec(memory_space=pltpu.VMEM),
        out_shape=jax.ShapeDtypeStruct((SESS, D), bf16),
        cost_estimate=pl.CostEstimate(flops=1 << 26, bytes_accessed=2 << 20, transcendentals=0),
        name="finish_keys",
    )(pointer, *parts)


def diagonal(n):
    return lax.broadcasted_iota(jnp.int32, (n, n), 0) == lax.broadcasted_iota(
        jnp.int32, (n, n), 1
    )


def to_row(col, eye):
    return jnp.sum(jnp.where(eye, jnp.broadcast_to(col, eye.shape), 0.0), axis=0, keepdims=True)


def to_col(row, eye):
    return jnp.sum(jnp.where(eye, jnp.broadcast_to(row, eye.shape), 0.0), axis=1, keepdims=True)


CHUNKS = ((0, 0, 512), (0, 512, 1536), (0, 2048, 2048), (0, 4096, 4096), (1, 0, 4096), (1, 4096, 4096))
SB = 512


def attend_kernel(loc_ref, q_ref, k0_ref, k1_ref, out_ref, kbuf, q2, m_ref, l_ref, acc, todo, sems):
    copies = []
    for n, (which, first, rows) in enumerate(CHUNKS):
        src = (k0_ref, k1_ref)[which]
        copy = pltpu.make_async_copy(
            src.at[pl.ds(first, rows)],
            kbuf.at[pl.ds(which * SLOTS + first, rows)],
            sems.at[n],
        )
        copy.start()
        copies.append((which * SLOTS + first, copy))
    for j in range(4):
        q2[j * OWN : (j + 1) * OWN, :] = q_ref[j, :OWN, :]

    def score(b):
        return lax.dot_general(
            q2[...], kbuf[b : b + SB, :], CONTRACT_LAST, preferred_element_type=f32
        )

    copies[0][1].wait()
    s = score(0)
    m_ref[...] = jnp.broadcast_to(jnp.max(s, axis=1, keepdims=True) * C2, (GRP, 128))
    l_ref[...] = jnp.zeros_like(l_ref)
    acc[...] = jnp.zeros_like(acc)
    waiting = copies[1:]
    total = 2 * SLOTS
    for b in range(0, total, SB):
        if b + SB < total:
            if waiting and waiting[0][0] == b + SB:
                waiting.pop(0)[1].wait()
            following = score(b + SB)
        m = m_ref[...]
        l = l_ref[...]
        ps = []
        for j in range(0, SB, 128):
            p = jnp.exp2(s[:, j : j + 128] * C2 - m)
            l = l + p
            ps.append(p.astype(bf16))
        l_ref[...] = l
        acc[...] += jnp.dot(
            jnp.concatenate(ps, axis=1), kbuf[b : b + SB, :], preferred_element_type=f32
        )
        s = following

    @pl.when(jnp.logical_not(jnp.max(l_ref[...]) < BIG))
    def _():
        m_ref[...] = jnp.full_like(m_ref, -3.0e38)
        l_ref[...] = jnp.zeros_like(l_ref)
        acc[...] = jnp.zeros_like(acc)

        def again(n, carry):
            block = kbuf[pl.ds(pl.multiple_of(n * SB, SB), SB), :]
            t = lax.dot_general(q2[...], block, CONTRACT_LAST, preferred_element_type=f32) * C2
            old = m_ref[...]
            new = jnp.maximum(old, jnp.max(t, axis=1, keepdims=True))
            keep = jnp.exp2(old - new)
            p = jnp.exp2(t - new[:, :1])
            part = p[:, :128]
            for j in range(128, SB, 128):
                part = part + p[:, j : j + 128]
            l_ref[...] = l_ref[...] * keep + part
            acc[...] = acc[...] * keep[:, :1] + jnp.dot(
                p.astype(bf16), block, preferred_element_type=f32
            )
            m_ref[...] = new
            return carry

        lax.fori_loop(0, total // SB, again, 0)

    eye = diagonal(OWN)
    lane_pad = jnp.zeros((1, D - OWN), f32)
    for j in range(4):
        rows = slice(j * OWN, (j + 1) * OWN)
        out_ref[j, :OWN, :] = acc[rows, :]
        m_row = to_row(m_ref[rows, :1], eye)
        l_row = to_row(jnp.sum(l_ref[rows, :], axis=1, keepdims=True), eye)
        out_ref[j, ML:POS, :] = jnp.concatenate(
            [
                jnp.concatenate([m_row, lane_pad], axis=1),
                jnp.concatenate([l_row, lane_pad], axis=1),
                jnp.zeros((6, D), f32),
            ],
            axis=0,
        )
        out_ref[j, POS:PIECE, :] = jnp.zeros((OWN, D), f32)

    def note(i, n):
        t = loc_ref[i]
        todo[n] = t * GRP + i
        return n + jnp.where(t >= 0, 1, 0)

    count = lax.fori_loop(0, GRP, note, 0, unroll=8)

    def fetch(j, carry):
        entry = todo[j]
        i = entry & (GRP - 1)
        t = entry >> 8
        group = kbuf[pl.ds(pl.multiple_of((t >> 4) << 4, 16), 16), :].astype(f32)
        hit = lax.broadcasted_iota(jnp.int32, (16, D), 0) == (t & 15)
        out_ref[i >> 6, pl.ds(POS + (i & 63), 1), :] = jnp.sum(
            jnp.where(hit, group, 0.0), axis=0, keepdims=True
        )
        return carry

    lax.fori_loop(0, count, fetch, 0)


def attend(loc, q, k_own, k_other):
    return pl.pallas_call(
        attend_kernel,
        in_specs=[
            pl.BlockSpec(memory_space=pltpu.SMEM),
            pl.BlockSpec(memory_space=pltpu.VMEM),
            pl.BlockSpec(memory_space=pl.ANY),
            pl.BlockSpec(memory_space=pl.ANY),
        ],
        out_specs=pl.BlockSpec(memory_space=pltpu.VMEM),
        out_shape=jax.ShapeDtypeStruct((4, PIECE, D), f32),
        scratch_shapes=[
            pltpu.VMEM((2 * SLOTS, D), bf16),
            pltpu.VMEM((GRP, D), bf16),
            pltpu.VMEM((GRP, 128), f32),
            pltpu.VMEM((GRP, 128), f32),
            pltpu.VMEM((GRP, D), f32),
            pltpu.SMEM((GRP + 8,), jnp.int32),
            pltpu.SemaphoreType.DMA((len(CHUNKS),)),
        ],
        compiler_params=pltpu.CompilerParams(vmem_limit_bytes=VMEM_LIMIT),
        cost_estimate=pl.CostEstimate(
            flops=8 * GRP * SLOTS * D, bytes_accessed=9 << 20, transcendentals=2 * GRP * SLOTS
        ),
        name="attend",
    )(loc, q, k_own, k_other)


def combine(pieces, eye):
    ms = [p[ML : ML + 1, :OWN] for p in pieces]
    top = functools.reduce(jnp.maximum, ms)
    scales = [jnp.exp2(m - top) for m in ms]
    total = sum(p[ML + 1 : ML + 2, :OWN] * s for p, s in zip(pieces, scales))
    return top, scales, total


def merge_kernel(a_ref, b_ref, c_ref, d_ref, *outs):
    eye = diagonal(OWN)
    lane_pad = jnp.zeros((1, D - OWN), f32)
    for j in range(4):
        refs = [r.at[j] for r in (a_ref, b_ref, c_ref, d_ref)]
        top, scales, total = combine(refs, eye)
        o = outs[j]
        o[:OWN, :] = sum(r[:OWN, :] * to_col(s, eye) for r, s in zip(refs, scales))
        o[ML:POS, :] = jnp.concatenate(
            [
                jnp.concatenate([top, lane_pad], axis=1),
                jnp.concatenate([total, lane_pad], axis=1),
                jnp.zeros((6, D), f32),
            ],
            axis=0,
        )
        o[POS:PIECE, :] = sum(r[POS:PIECE, :] for r in refs)


def merge(states):
    return pl.pallas_call(
        merge_kernel,
        in_specs=[pl.BlockSpec(memory_space=pltpu.VMEM)] * 4,
        out_specs=[pl.BlockSpec(memory_space=pltpu.VMEM)] * 4,
        out_shape=[jax.ShapeDtypeStruct((PIECE, D), f32)] * 4,
        compiler_params=pltpu.CompilerParams(vmem_limit_bytes=VMEM_LIMIT),
        cost_estimate=pl.CostEstimate(flops=1 << 22, bytes_accessed=3 << 20, transcendentals=4096),
        name="merge",
    )(*states)


def final_kernel(q_ref, a_ref, b_ref, c_ref, d_ref, loss_ref, grad_ref):
    eye = diagonal(OWN)
    refs = (a_ref, b_ref, c_ref, d_ref)
    top, scales, total = combine(refs, eye)
    inverse = 1.0 / total
    acc = sum(r[:OWN, :] * to_col(s * inverse, eye) for r, s in zip(refs, scales))
    positive = sum(r[POS:PIECE, :] for r in refs)
    grad_ref[...] = SOFT * (acc - positive)
    score = SOFT * jnp.sum(q_ref[...].astype(f32) * positive, axis=1, keepdims=True)
    loss_ref[...] = top * LN2 + jnp.log(total) - to_row(score, eye)


def finish(q, pieces):
    loss, grad = pl.pallas_call(
        final_kernel,
        in_specs=[pl.BlockSpec(memory_space=pltpu.VMEM)] * 5,
        out_specs=[pl.BlockSpec(memory_space=pltpu.VMEM)] * 2,
        out_shape=[jax.ShapeDtypeStruct((1, OWN), f32), jax.ShapeDtypeStruct((OWN, D), f32)],
        cost_estimate=pl.CostEstimate(flops=1 << 20, bytes_accessed=1 << 20, transcendentals=1024),
        name="finish",
    )(q, *pieces)
    return loss.reshape(OWN), grad


BLK = SESS
NBLK = SLOTS // BLK


def memory_kernel(info_ref, keys_ref, k_ref, out_ref, rbuf, kbuf, obuf, gsem, ksem, osem):
    pointer, me = info_ref[0], info_ref[1]
    r = lax.rem(pointer, SLOTS)
    first = lax.div(pointer, SLOTS)
    second = lax.rem(first + 1, 32)
    turn = lax.div(r, BLK)
    inner = lax.rem(r, BLK)
    is_first, is_second = me == first, me == second

    def needs_new(b):
        return jnp.logical_or(
            jnp.logical_and(is_first, (b + 1) * BLK > r), jnp.logical_and(is_second, b * BLK < r)
        )

    def needs_old(b):
        return jnp.logical_not(
            jnp.logical_or(
                jnp.logical_and(is_first, b * BLK >= r),
                jnp.logical_and(is_second, (b + 1) * BLK <= r),
            )
        )

    def new_copy(slot):
        block = lax.rem(slot - 1 - turn + 2 * NBLK, NBLK)
        return pltpu.make_async_copy(
            keys_ref.at[pl.ds(pl.multiple_of(block * BLK, BLK), BLK)],
            rbuf.at[pl.ds(slot * BLK, BLK)],
            gsem.at[slot],
        )

    def new_wanted(slot):
        wanted = []
        if slot > 0:
            wanted.append(needs_new(slot - 1))
        if slot < NBLK:
            wanted.append(needs_new(slot))
        return functools.reduce(jnp.logical_or, wanted)

    def old_copy(b):
        rows = pl.ds(b * BLK, BLK)
        return pltpu.make_async_copy(k_ref.at[rows], kbuf.at[rows], ksem.at[b])

    def out_copy(b):
        rows = pl.ds(b * BLK, BLK)
        return pltpu.make_async_copy(obuf.at[rows], out_ref.at[rows], osem.at[b])

    for slot in range(NBLK + 1):

        @pl.when(new_wanted(slot))
        def _():
            new_copy(slot).start()

        if slot < NBLK:

            @pl.when(needs_old(slot))
            def _():
                old_copy(slot).start()

    @pl.when(new_wanted(0))
    def _():
        new_copy(0).wait()

    row = lax.broadcasted_iota(jnp.int32, (BLK, D), 0)
    for b in range(NBLK):

        @pl.when(new_wanted(b + 1))
        def _():
            new_copy(b + 1).wait()

        @pl.when(needs_old(b))
        def _():
            old_copy(b).wait()

        rows = slice(b * BLK, (b + 1) * BLK)

        @pl.when(needs_new(b))
        def _():
            earlier = row < inner
            at = row + b * BLK
            take = jnp.logical_or(
                jnp.logical_and(is_first, at >= r), jnp.logical_and(is_second, at < r)
            )
            fresh = jnp.where(
                earlier,
                rbuf[rows, :].astype(f32),
                rbuf[(b + 1) * BLK : (b + 2) * BLK, :].astype(f32),
            )
            obuf[rows, :] = jnp.where(take, fresh, kbuf[rows, :].astype(f32)).astype(bf16)

        @pl.when(jnp.logical_not(needs_new(b)))
        def _():
            obuf[rows, :] = kbuf[rows, :]

        out_copy(b).start()
    for b in range(NBLK):
        out_copy(b).wait()


def new_memory_of(info, keys, key_queue):
    anywhere = pl.BlockSpec(memory_space=pl.ANY)
    return pl.pallas_call(
        memory_kernel,
        in_specs=[pl.BlockSpec(memory_space=pltpu.SMEM), anywhere, anywhere],
        out_specs=anywhere,
        out_shape=jax.ShapeDtypeStruct((SLOTS, D), bf16),
        scratch_shapes=[
            pltpu.VMEM((SLOTS + BLK, D), bf16),
            pltpu.VMEM((SLOTS, D), bf16),
            pltpu.VMEM((SLOTS, D), bf16),
            pltpu.SemaphoreType.DMA((NBLK + 1,)),
            pltpu.SemaphoreType.DMA((NBLK,)),
            pltpu.SemaphoreType.DMA((NBLK,)),
        ],
        compiler_params=pltpu.CompilerParams(vmem_limit_bytes=VMEM_LIMIT),
        cost_estimate=pl.CostEstimate(flops=1 << 22, bytes_accessed=12 << 20, transcendentals=0),
        name="new_memory",
    )(info, keys, key_queue)


def with_targets(probe, target):
    digits = jnp.stack([target & 255, (target >> 8) & 255, target >> 16]).astype(bf16)
    digits = jnp.pad(digits, ((0, 13), (0, D - OWN)))
    return jnp.concatenate([probe, digits], axis=0)


def local_targets(q, first, core):
    d = q[:, OWN : OWN + 3, :OWN].astype(jnp.int32)
    t = d[:, 0] + d[:, 1] * 256 + d[:, 2] * 65536 - first
    t = jnp.where((t >= 0) & (t < 2 * SLOTS), t ^ (core * SLOTS), -1)
    return t.reshape(GRP)


def shards(events, w_in, w_out, probe, key_queue, target, pointer):
    core = lax.axis_index("c")
    chip = lax.axis_index("x") * SIZES[1] + lax.axis_index("z")
    first_slot = chip * (2 * SLOTS)

    q = with_targets(probe, target)
    partial = encode(events, w_in, w_out)
    k_other = swap_cores(key_queue)
    near = jnp.stack([q] + [shift(q, "zx", j) for j in (1, 2, 3)])
    parts = [partial] + [shift(partial, "ff", j) for j in (1, 3, 2)]
    far = [shift(near, "xz", j) for j in (1, 3, 2)]

    parts, near = lax.optimization_barrier((parts, near))
    far = [shift(near, "xz", j) for j in (1, 3, 2)]
    rolled = finish_keys(pointer, parts)
    all_keys = lax.all_gather(rolled, ("x", "z", "c"), axis=0, tiled=True)

    states = []
    for group in far + [near]:
        loc = local_targets(group, first_slot, core)
        if states:
            group, loc, states[-1] = lax.optimization_barrier((group, loc, states[-1]))
        states.append(attend(loc, group, key_queue, k_other))
    back = [shift(state, "xz", -j) for state, j in zip(states, (1, 3, 2))]
    pieces = merge([states[-1]] + back)
    arrived = [pieces[0]] + [shift(pieces[j], "zx", -j) for j in (1, 3, 2)]
    loss, grad = finish(probe, arrived)

    info = jnp.stack([pointer[0], chip * 2 + core]).astype(jnp.int32)
    new_memory = new_memory_of(info, all_keys, key_queue)
    return loss, grad, new_memory


def solution(mesh):
    fine = Mesh(mesh.devices.reshape(SIZES), ALL)
    mem = ("x", "z", "c")
    return jax.shard_map(
        shards,
        mesh=fine,
        in_specs=(
            P(mem, None, None),
            P(None, "f"),
            P("f", None),
            P(ALL, None),
            P(mem, None),
            P(ALL),
            P(),
        ),
        out_specs=(P(ALL), P(ALL, None), P(mem, None)),
        check_vma=False,
    )
```

time: 588 us -> 119 us (0.20)
  blocking collectives: 201 us -> 0 us
  waiting for transfers between devices: 167 us -> 21.3 us
  matrix products: 94.4 us -> 0 us
  other arithmetic: 57.2 us -> 0.25 us
  Pallas kernels: 0 us -> 51.4 us
  local copies, waits for them, and re-layouts: 50.4 us -> 4.21 us
  starting transfers between devices: 0.17 us -> 25.2 us
    psum x1 -> x0, blocking collectives: 121 us -> none  [shards(): lax.psum((local_sum * jnp.exp(local_max - top), local_score), 'mem')]
    psum x2 -> x0, waiting for transfers between devices: 104 us -> none  [the longest x1 104 us: shards(): lax.psum(inverse_softness * (collected_denominator - paired_entries), 'mem')]
    dot_general x18 -> x0, matrix products: 94.4 us -> none  [the longest x8 47.2 us: slot_scores(): lax.dot_general(query_rows, queue_position_span, (((1,), (1,)), ((), ()))...]
    pmax x1 -> x0, blocking collectives: 63.2 us -> none  [shards(): top = lax.pmax(local_max, 'mem')]
    all_gather x2 -> x1, waiting for transfers between devices: 62.2 us -> 0.01 us  [shards(): all_keys = lax.all_gather(rolled, ('x', 'z', 'c'), axis=0, tiled=True)]
    pallas_call x0 -> x9, Pallas kernels: none -> 51.4 us  [the longest x4 34.6 us: attend(): pl.pallas_call(attend_kernel, in_specs=[pl.BlockSpec(memory_space=pltpu.S...]
    gather x2 -> x0, local copies, waits for them, and re-layouts: 43.3 us -> none  [the longest x1 33.9 us: shards(): picked = jnp.take(keys_all, jnp.minimum(offsets, session_count - 1), axis=0)]
    reduce_sum x9 -> x0, other arithmetic: 38.7 us -> none  [the longest x8 37.6 us: first_pass(): jnp.sum(jnp.where(hit, similarity_table, 0.0), axis=1)]
  transfers between devices with their start and end apart: 4 -> 17, of which waited for: 3 -> 9; matrix products, arithmetic and copies ran while one was open for 27% -> 0% of each run, Pallas kernels for 0% -> 31%
where the time goes in v1:
time: 119 us; the launch traced here: 117 us
  Pallas kernels  51.4 us (43%)
  starting transfers between devices  25.2 us (21%)
  waiting for transfers between devices  21.3 us (18%)
  between operations  14.9 us (13%)
  local copies, waits for them, and re-layouts  4.21 us (4%)
    pallas_call x4, Pallas kernels, attend(): pl.pallas_call(attend_kernel, in_specs=[pl.BlockSpec(memory_space=pltpu.S...  34.6 us
    ppermute x15, starting transfers between devices, shift(): return lax.ppermute(a, ALL, ring(axes, step % 4))  23.4 us
    ppermute x15, waiting for transfers between devices, shift(): return lax.ppermute(a, ALL, ring(axes, step % 4))  21.3 us
    pallas_call x1, Pallas kernels, encode(): pl.pallas_call(encoder_kernel, grid=(SESS // step,), in_specs=[pl.BlockSp...  7.08 us
    pallas_call x1, Pallas kernels, new_memory_of(): pl.pallas_call(memory_kernel, in_specs=[pl.BlockSpec(memory_space=pltpu.S...  5.4 us
    unnamed x24, local copies, waits for them, and re-layouts  3.88 us
  transfers between devices with their start and end apart: 17, of which 9 were waited for; matrix products, arithmetic and copies ran while one was open for 0% of the time, Pallas kernels for 31%

profile of v1, /device:TPU:1, one launch (start us, length us, event | category | flops | bytes accessed | tf_op | source)
XLA Modules:
  0.0 117.2 jit_solution(6565966962842973463)
XLA Ops:
  7.2 0.0 all-gather.2.cloned.1.call-start
  7.2 0.0 copy-start.2
  7.2 0.9 copy-done.2
  8.1 0.9 copy-done.3
  9.0 7.1 %encoder.1.a_ref = f32[256,256]{1,0:T(8,128)S(1)} custom-call(bf16[256,32,256]{2,1,0:T(8,128)(2,1)} %ev_ref.1, bf16[256,256]{1,0:T(8,128)(2,1)S(1)} %copy-done.2, bf16[256,256]{1,0:T(8,128)(2,1)S(1)} %copy-done.3), custom_call_target="tpu_custom_call" | custom-call | flops 1073741824 | bytes 4194304 | tf_op jit(solution)/shard_map/encoder/pallas_call | solution.py:82
  16.1 0.0 copy-start
  16.1 2.2 %collective-permute-start = (f32[256,256]{1,0:T(8,128)S(1)}, f32[256,256]{1,0:T(8,128)S(1)}, u32[]{:S(2)}, u32[]{:S(2)}) collective-permute-start(f32[256,256]{1,0:T(8,128)S(1)} %encoder.1.a_ref), channel_id=1, source_target_pairs={{0,1},{1,2},{2,3},{3,0},{4,5},{5,6},{6,7},{7,4},{8,9},{9,10},{10,1... | collective-permute-start | bytes 786440 | tf_op jit(solution)/shard_map/ppermute | solution.py:52
  18.3 1.5 %collective-permute-start.1 = (f32[256,256]{1,0:T(8,128)S(1)}, f32[256,256]{1,0:T(8,128)S(1)}, u32[]{:S(2)}, u32[]{:S(2)}) collective-permute-start(f32[256,256]{1,0:T(8,128)S(1)} %encoder.1.a_ref), channel_id=1, source_target_pairs={{0,3},{1,0},{2,1},{3,2},{4,7},{5,4},{6,5},{7,6},{8,11},{9,8},{10,9... | collective-permute-start | bytes 786440 | tf_op jit(solution)/shard_map/ppermute | solution.py:52
  19.8 1.6 %collective-permute-start.2 = (f32[256,256]{1,0:T(8,128)S(1)}, f32[256,256]{1,0:T(8,128)S(1)}, u32[]{:S(2)}, u32[]{:S(2)}) collective-permute-start(f32[256,256]{1,0:T(8,128)S(1)} %encoder.1.a_ref), channel_id=1, source_target_pairs={{0,2},{1,3},{2,0},{3,1},{4,6},{5,7},{6,4},{7,5},{8,10},{9,11},{10,... | collective-permute-start | bytes 786440 | tf_op jit(solution)/shard_map/ppermute | solution.py:52
  21.4 0.0 copy-done.11
  21.4 0.0 copy-done.10
  21.4 1.3 %collective-permute-start.3 = (bf16[80,256]{1,0:T(8,128)(2,1)S(1)}, bf16[80,256]{1,0:T(8,128)(2,1)S(1)}, u32[]{:S(2)}, u32[]{:S(2)}) collective-permute-start(bf16[80,256]{1,0:T(8,128)(2,1)S(1)} %get-tuple-element.44), channel_id=1, source_target_pairs={{0,8},{1,9},{2,10},{3,11},{4,36},{5,37},{6,38},{7,39},{8,16},{9,17... | collective-permute-start | bytes 122888 | tf_op jit(solution)/shard_map/ppermute | solution.py:52
  22.7 2.5 %collective-permute-start.4 = (bf16[80,256]{1,0:T(8,128)(2,1)S(1)}, bf16[80,256]{1,0:T(8,128)(2,1)S(1)}, u32[]{:S(2)}, u32[]{:S(2)}) collective-permute-start(bf16[80,256]{1,0:T(8,128)(2,1)S(1)} %get-tuple-element.44), channel_id=1, source_target_pairs={{0,16},{1,17},{2,18},{3,19},{4,68},{5,69},{6,70},{7,71},{8,24},{9,... | collective-permute-start | bytes 122888 | tf_op jit(solution)/shard_map/ppermute | solution.py:52
  25.2 0.7 collective-permute-done.3
  25.9 1.3 %collective-permute-start.5 = (bf16[80,256]{1,0:T(8,128)(2,1)S(1)}, bf16[80,256]{1,0:T(8,128)(2,1)S(1)}, u32[]{:S(2)}, u32[]{:S(2)}) collective-permute-start(bf16[80,256]{1,0:T(8,128)(2,1)S(1)} %get-tuple-element.44), channel_id=1, source_target_pairs={{0,24},{1,25},{2,26},{3,27},{4,100},{5,101},{6,102},{7,103},{8,0},... | collective-permute-start | bytes 122888 | tf_op jit(solution)/shard_map/ppermute | solution.py:52
  27.8 0.0 collective-permute-done.4
  27.8 1.2 %collective-permute-done.5 = bf16[80,256]{1,0:T(8,128)(2,1)S(1)} collective-permute-done((bf16[80,256]{1,0:T(8,128)(2,1)S(1)}, bf16[80,256]{1,0:T(8,128)(2,1)S(1)}, u32[]{:S(2)}, u32[]{:S(2)}) %collective-permute-start.5) | collective-permute-done | bytes 40992 | tf_op jit(solution)/shard_map/ppermute | solution.py:52
  29.1 0.0 collective-permute-done.b_ref
  29.1 0.0 copy-start.4
  29.1 0.0 collective-permute-done.1.c_ref
  29.1 0.0 copy-start.5
  29.1 3.2 %collective-permute-done.2.d_ref = f32[256,256]{1,0:T(8,128)S(1)} collective-permute-done((f32[256,256]{1,0:T(8,128)S(1)}, f32[256,256]{1,0:T(8,128)S(1)}, u32[]{:S(2)}, u32[]{:S(2)}) %collective-permute-start.2) | collective-permute-done | bytes 262176 | tf_op jit(solution)/shard_map/ppermute | solution.py:52
  32.3 0.0 copy-done
  32.3 0.0 copy-done.4
  32.3 0.0 copy-done.5
  32.3 0.7 copy-done.6
  33.0 2.1 %finish_keys.1 = bf16[256,256]{1,0:T(8,128)(2,1)} custom-call(s32[1]{0:T(128)S(6)} %copy.10.ptr_ref, f32[256,256]{1,0:T(8,128)} %copy-done, f32[256,256]{1,0:T(8,128)} %copy-done.4, f32[256,256]{1,0:T(8,128)} %copy-done.5, f32[256,256]{1,0:T(8,128)} %copy-done.6), custom_call_target="tpu_custom_call" | custom-call | flops 67108864 | bytes 2097152 | tf_op jit(solution)/shard_map/finish_keys/pallas_call | solution.py:115
  35.1 0.0 all-gather.2.cloned.1.call-update
  35.1 1.7 %collective-permute-start.9 = (bf16[8192,256]{1,0:T(8,128)(2,1)}, bf16[8192,256]{1,0:T(8,128)(2,1)}, u32[]{:S(2)}, u32[]{:S(2)}) collective-permute-start(bf16[8192,256]{1,0:T(8,128)(2,1)} %k_ref.1), channel_id=1, source_target_pairs={{0,4},{4,0},{1,5},{5,1},{2,6},{6,2},{3,7},{7,3},{8,12},{12,8},{9,1... | collective-permute-start | bytes 12582920 | tf_op jit(solution)/shard_map/ppermute | solution.py:56
  36.8 1.6 %collective-permute-start.8 = (bf16[4,80,256]{2,1,0:T(8,128)(2,1)S(1)}, bf16[4,80,256]{2,1,0:T(8,128)(2,1)S(1)}, u32[]{:S(2)}, u32[]{:S(2)}) collective-permute-start(bf16[4,80,256]{2,1,0:T(8,128)(2,1)S(1)} %pad_maximum_fusion.q_ref), channel_id=1, source_target_pairs={{0,32},{1,33},{2,34},{3,35},{4,12},{5,13},{6,14},{7,15},{8,40},{9,... | collective-permute-start | bytes 491528 | tf_op jit(solution)/shard_map/ppermute | solution.py:52
  38.4 3.3 %collective-permute-start.6 = (bf16[4,80,256]{2,1,0:T(8,128)(2,1)S(1)}, bf16[4,80,256]{2,1,0:T(8,128)(2,1)S(1)}, u32[]{:S(2)}, u32[]{:S(2)}) collective-permute-start(bf16[4,80,256]{2,1,0:T(8,128)(2,1)S(1)} %pad_maximum_fusion.q_ref), channel_id=1, source_target_pairs={{0,64},{1,65},{2,66},{3,67},{4,20},{5,21},{6,22},{7,23},{8,72},{9,... | collective-permute-start | bytes 491528 | tf_op jit(solution)/shard_map/ppermute | solution.py:52
  41.7 0.7 collective-permute-start.7
  42.5 0.1 reshape.87.loc_ref
  42.6 0.7 collective-permute-done.8.q_ref
  43.2 2.9 %collective-permute-done.6.q_ref = bf16[4,80,256]{2,1,0:T(8,128)(2,1)S(1)} collective-permute-done((bf16[4,80,256]{2,1,0:T(8,128)(2,1)S(1)}, bf16[4,80,256]{2,1,0:T(8,128)(2,1)S(1)}, u32[]{:S(2)}, u32[]{:S(2)}) %collective-permute-start.6) | collective-permute-done | bytes 163872 | tf_op jit(solution)/shard_map/ppermute | solution.py:52
  46.2 0.1 reshape.93.loc_ref
  46.3 0.0 collective-permute-done.7.q_ref
  46.3 0.1 reshape.91.loc_ref
  46.4 0.1 reshape.89.loc_ref
  46.5 0.0 collective-permute-done.9.k1_ref
  46.5 8.8 %attend.4 = f32[4,136,256]{2,1,0:T(8,128)S(1)} custom-call(s32[256]{0:T(256)S(1)} %reshape.93.loc_ref, bf16[4,80,256]{2,1,0:T(8,128)(2,1)S(1)} %collective-permute-done.8.q_ref, bf16[8192,256]{1,0:T(8,128)(2,1)} %k_ref.1, bf16[8192,256]{1,0:T(8,128)(2,1)} %collective-permute-done.9.k1_ref), custom_call_target="tpu_custom_call" | custom-call | flops 4294967296 | bytes 9437184 | tf_op jit(solution)/shard_map/attend/pallas_call | solution.py:252
  55.3 8.6 %attend.5 = f32[4,136,256]{2,1,0:T(8,128)S(1)} custom-call(s32[256]{0:T(256)S(1)} %reshape.91.loc_ref, bf16[4,80,256]{2,1,0:T(8,128)(2,1)S(1)} %collective-permute-done.7.q_ref, bf16[8192,256]{1,0:T(8,128)(2,1)} %k_ref.1, bf16[8192,256]{1,0:T(8,128)(2,1)} %collective-permute-done.9.k1_ref), custom_call_target="tpu_custom_call" | custom-call | flops 4294967296 | bytes 9437184 | tf_op jit(solution)/shard_map/attend/pallas_call | solution.py:252
  63.9 8.5 %attend.6 = f32[4,136,256]{2,1,0:T(8,128)S(1)} custom-call(s32[256]{0:T(256)S(1)} %reshape.89.loc_ref, bf16[4,80,256]{2,1,0:T(8,128)(2,1)S(1)} %collective-permute-done.6.q_ref, bf16[8192,256]{1,0:T(8,128)(2,1)} %k_ref.1, bf16[8192,256]{1,0:T(8,128)(2,1)} %collective-permute-done.9.k1_ref), custom_call_target="tpu_custom_call" | custom-call | flops 4294967296 | bytes 9437184 | tf_op jit(solution)/shard_map/attend/pallas_call | solution.py:252
  72.5 2.3 %collective-permute-start.12 = (f32[4,136,256]{2,1,0:T(8,128)S(1)}, f32[4,136,256]{2,1,0:T(8,128)S(1)}, u32[]{:S(2)}, u32[]{:S(2)}) collective-permute-start(f32[4,136,256]{2,1,0:T(8,128)S(1)} %attend.6), channel_id=1, source_target_pairs={{0,64},{1,65},{2,66},{3,67},{4,20},{5,21},{6,22},{7,23},{8,72},{9,... | collective-permute-start | bytes 1671176 | tf_op jit(solution)/shard_map/ppermute | solution.py:52
  74.8 0.3 collective-permute-start.11
  75.1 2.4 %collective-permute-start.10 = (f32[4,136,256]{2,1,0:T(8,128)S(1)}, f32[4,136,256]{2,1,0:T(8,128)S(1)}, u32[]{:S(2)}, u32[]{:S(2)}) collective-permute-start(f32[4,136,256]{2,1,0:T(8,128)S(1)} %attend.4), channel_id=1, source_target_pairs={{0,96},{1,97},{2,98},{3,99},{4,28},{5,29},{6,30},{7,31},{8,104},{9... | collective-permute-start | bytes 1671176 | tf_op jit(solution)/shard_map/ppermute | solution.py:52
  77.5 8.7 %attend.7.a_ref = f32[4,136,256]{2,1,0:T(8,128)S(1)} custom-call(s32[256]{0:T(256)S(1)} %reshape.87.loc_ref, bf16[4,80,256]{2,1,0:T(8,128)(2,1)S(1)} %pad_maximum_fusion.q_ref, bf16[8192,256]{1,0:T(8,128)(2,1)} %k_ref.1, bf16[8192,256]{1,0:T(8,128)(2,1)} %collective-permute-done.9.k1_ref), custom_call_target="tpu_custom_call" | custom-call | flops 4294967296 | bytes 9437184 | tf_op jit(solution)/shard_map/attend/pallas_call | solution.py:252
  86.2 1.4 %collective-permute-done.12.d_ref = f32[4,136,256]{2,1,0:T(8,128)S(1)} collective-permute-done((f32[4,136,256]{2,1,0:T(8,128)S(1)}, f32[4,136,256]{2,1,0:T(8,128)S(1)}, u32[]{:S(2)}, u32[]{:S(2)}) %collective-permute-start.12) | collective-permute-done | bytes 557088 | tf_op jit(solution)/shard_map/ppermute | solution.py:52
  87.5 5.9 %collective-permute-done.11.c_ref = f32[4,136,256]{2,1,0:T(8,128)S(1)} collective-permute-done((f32[4,136,256]{2,1,0:T(8,128)S(1)}, f32[4,136,256]{2,1,0:T(8,128)S(1)}, u32[]{:S(2)}, u32[]{:S(2)}) %collective-permute-start.11) | collective-permute-done | bytes 557088 | tf_op jit(solution)/shard_map/ppermute | solution.py:52
  93.4 0.0 collective-permute-done.10.b_ref
  93.4 0.2 merge.1
  93.6 0.0 copy-start.1
  93.6 0.6 copy-done.1
  94.3 1.1 collective-permute-start.13
  95.4 0.3 collective-permute-start.14
  95.8 1.1 collective-permute-start.15
  96.9 0.1 pad_add_fusion.info_ref
  96.9 1.3 %collective-permute-done.13.b_ref = f32[136,256]{1,0:T(8,128)S(1)} collective-permute-done((f32[136,256]{1,0:T(8,128)S(1)}, f32[136,256]{1,0:T(8,128)S(1)}, u32[]{:S(2)}, u32[]{:S(2)}) %collective-permute-start.13) | collective-permute-done | bytes 139296 | tf_op jit(solution)/shard_map/ppermute | solution.py:52
  98.2 4.1 %collective-permute-done.14.c_ref = f32[136,256]{1,0:T(8,128)S(1)} collective-permute-done((f32[136,256]{1,0:T(8,128)S(1)}, f32[136,256]{1,0:T(8,128)S(1)}, u32[]{:S(2)}, u32[]{:S(2)}) %collective-permute-start.14) | collective-permute-done | bytes 139296 | tf_op jit(solution)/shard_map/ppermute | solution.py:52
  102.3 0.0 collective-permute-done.15.d_ref
  102.3 0.6 copy-done.8
  103.0 0.1 copy-done.9
  103.1 1.9 %finish.1 = (f32[1,64]{1,0:T(1,128)}, f32[64,256]{1,0:T(8,128)}) custom-call(bf16[64,256]{1,0:T(8,128)(2,1)} %q_ref.1, f32[136,256]{1,0:T(8,128)} %copy-done.1, f32[136,256]{1,0:T(8,128)} %copy-done.7, f32[136,256]{1,0:T(8,128)} %copy-done.8, f32[136,256]{1,0:T(8,128)} %copy-done.9), custom_call_target="tpu_custom_call" | custom-call | flops 1048576 | bytes 1048576 | tf_op jit(solution)/shard_map/finish/pallas_call | solution.py:331
  105.0 5.4 %new_memory.1 = bf16[8192,256]{1,0:T(8,128)(2,1)} custom-call(s32[2]{0:T(128)S(1)} %pad_add_fusion.info_ref, bf16[8192,256]{1,0:T(8,128)(2,1)} %all-gather.2.cloned.1.call-done.keys_ref, bf16[8192,256]{1,0:T(8,128)(2,1)} %k_ref.1), custom_call_target="tpu_custom_call" | custom-call | flops 4194304 | bytes 12582912 | tf_op jit(solution)/shard_map/new_memory/pallas_call | solution.py:446
  (20 shorter events, 0.2 us)
Async XLA Ops:
  7.2 97.8 %all-gather.2.cloned.1.call-start = ((), (), s32[]{:S(2)}) async-start(), calls=%async_computation | async-start | bytes 4325376 | tf_op jit(solution)/shard_map/all_gather | solution.py:493
  7.2 0.9 copy-start.2
  8.1 0.9 copy-start.3
  9.0 12.4 %copy-start.11 = (s32[64]{0:T(128)S(1)}, s32[64]{0:T(128)}, u32[]{:S(2)}) copy-start(s32[64]{0:T(128)} %param.12) | copy-start | bytes 772
  9.0 12.4 %copy-start.10 = (bf16[64,256]{1,0:T(8,128)(2,1)S(1)}, bf16[64,256]{1,0:T(8,128)(2,1)}, u32[]{:S(2)}) copy-start(bf16[64,256]{1,0:T(8,128)(2,1)} %q_ref.1) | copy-start | bytes 98308
  16.1 16.2 %copy-start = (f32[256,256]{1,0:T(8,128)}, f32[256,256]{1,0:T(8,128)S(1)}, u32[]{:S(2)}) copy-start(f32[256,256]{1,0:T(8,128)S(1)} %encoder.1.a_ref) | copy-start | bytes 786436
  16.1 12.9 %collective-permute-start = (f32[256,256]{1,0:T(8,128)S(1)}, f32[256,256]{1,0:T(8,128)S(1)}, u32[]{:S(2)}, u32[]{:S(2)}) collective-permute-start(f32[256,256]{1,0:T(8,128)S(1)} %encoder.1.a_ref), channel_id=1, source_target_pairs={{0,1},{1,2},{2,3},{3,0},{4,5},{5,6},{6,7},{7,4},{8,9},{9,10},{10,1... | collective-permute-start | bytes 786440 | tf_op jit(solution)/shard_map/ppermute | solution.py:52
  18.3 10.8 %collective-permute-start.1 = (f32[256,256]{1,0:T(8,128)S(1)}, f32[256,256]{1,0:T(8,128)S(1)}, u32[]{:S(2)}, u32[]{:S(2)}) collective-permute-start(f32[256,256]{1,0:T(8,128)S(1)} %encoder.1.a_ref), channel_id=1, source_target_pairs={{0,3},{1,0},{2,1},{3,2},{4,7},{5,4},{6,5},{7,6},{8,11},{9,8},{10,9... | collective-permute-start | bytes 786440 | tf_op jit(solution)/shard_map/ppermute | solution.py:52
  19.8 12.4 %collective-permute-start.2 = (f32[256,256]{1,0:T(8,128)S(1)}, f32[256,256]{1,0:T(8,128)S(1)}, u32[]{:S(2)}, u32[]{:S(2)}) collective-permute-start(f32[256,256]{1,0:T(8,128)S(1)} %encoder.1.a_ref), channel_id=1, source_target_pairs={{0,2},{1,3},{2,0},{3,1},{4,6},{5,7},{6,4},{7,5},{8,10},{9,11},{10,... | collective-permute-start | bytes 786440 | tf_op jit(solution)/shard_map/ppermute | solution.py:52
  21.4 4.4 %collective-permute-start.3 = (bf16[80,256]{1,0:T(8,128)(2,1)S(1)}, bf16[80,256]{1,0:T(8,128)(2,1)S(1)}, u32[]{:S(2)}, u32[]{:S(2)}) collective-permute-start(bf16[80,256]{1,0:T(8,128)(2,1)S(1)} %get-tuple-element.44), channel_id=1, source_target_pairs={{0,8},{1,9},{2,10},{3,11},{4,36},{5,37},{6,38},{7,39},{8,16},{9,17... | collective-permute-start | bytes 122888 | tf_op jit(solution)/shard_map/ppermute | solution.py:52
  22.7 5.1 %collective-permute-start.4 = (bf16[80,256]{1,0:T(8,128)(2,1)S(1)}, bf16[80,256]{1,0:T(8,128)(2,1)S(1)}, u32[]{:S(2)}, u32[]{:S(2)}) collective-permute-start(bf16[80,256]{1,0:T(8,128)(2,1)S(1)} %get-tuple-element.44), channel_id=1, source_target_pairs={{0,16},{1,17},{2,18},{3,19},{4,68},{5,69},{6,70},{7,71},{8,24},{9,... | collective-permute-start | bytes 122888 | tf_op jit(solution)/shard_map/ppermute | solution.py:52
  25.9 3.1 %collective-permute-start.5 = (bf16[80,256]{1,0:T(8,128)(2,1)S(1)}, bf16[80,256]{1,0:T(8,128)(2,1)S(1)}, u32[]{:S(2)}, u32[]{:S(2)}) collective-permute-start(bf16[80,256]{1,0:T(8,128)(2,1)S(1)} %get-tuple-element.44), channel_id=1, source_target_pairs={{0,24},{1,25},{2,26},{3,27},{4,100},{5,101},{6,102},{7,103},{8,0},... | collective-permute-start | bytes 122888 | tf_op jit(solution)/shard_map/ppermute | solution.py:52
  29.1 3.2 %copy-start.4 = (f32[256,256]{1,0:T(8,128)}, f32[256,256]{1,0:T(8,128)S(1)}, u32[]{:S(2)}) copy-start(f32[256,256]{1,0:T(8,128)S(1)} %collective-permute-done.b_ref) | copy-start | bytes 786436
  29.1 3.2 %copy-start.5 = (f32[256,256]{1,0:T(8,128)}, f32[256,256]{1,0:T(8,128)S(1)}, u32[]{:S(2)}) copy-start(f32[256,256]{1,0:T(8,128)S(1)} %collective-permute-done.1.c_ref) | copy-start | bytes 786436
  32.3 0.7 copy-start.6
  35.1 11.4 %collective-permute-start.9 = (bf16[8192,256]{1,0:T(8,128)(2,1)}, bf16[8192,256]{1,0:T(8,128)(2,1)}, u32[]{:S(2)}, u32[]{:S(2)}) collective-permute-start(bf16[8192,256]{1,0:T(8,128)(2,1)} %k_ref.1), channel_id=1, source_target_pairs={{0,4},{4,0},{1,5},{5,1},{2,6},{6,2},{3,7},{7,3},{8,12},{12,8},{9,1... | collective-permute-start | bytes 12582920 | tf_op jit(solution)/shard_map/ppermute | solution.py:56
  36.8 6.4 %collective-permute-start.8 = (bf16[4,80,256]{2,1,0:T(8,128)(2,1)S(1)}, bf16[4,80,256]{2,1,0:T(8,128)(2,1)S(1)}, u32[]{:S(2)}, u32[]{:S(2)}) collective-permute-start(bf16[4,80,256]{2,1,0:T(8,128)(2,1)S(1)} %pad_maximum_fusion.q_ref), channel_id=1, source_target_pairs={{0,32},{1,33},{2,34},{3,35},{4,12},{5,13},{6,14},{7,15},{8,40},{9,... | collective-permute-start | bytes 491528 | tf_op jit(solution)/shard_map/ppermute | solution.py:52
  38.4 7.8 %collective-permute-start.6 = (bf16[4,80,256]{2,1,0:T(8,128)(2,1)S(1)}, bf16[4,80,256]{2,1,0:T(8,128)(2,1)S(1)}, u32[]{:S(2)}, u32[]{:S(2)}) collective-permute-start(bf16[4,80,256]{2,1,0:T(8,128)(2,1)S(1)} %pad_maximum_fusion.q_ref), channel_id=1, source_target_pairs={{0,64},{1,65},{2,66},{3,67},{4,20},{5,21},{6,22},{7,23},{8,72},{9,... | collective-permute-start | bytes 491528 | tf_op jit(solution)/shard_map/ppermute | solution.py:52
  41.7 4.6 %collective-permute-start.7 = (bf16[4,80,256]{2,1,0:T(8,128)(2,1)S(1)}, bf16[4,80,256]{2,1,0:T(8,128)(2,1)S(1)}, u32[]{:S(2)}, u32[]{:S(2)}) collective-permute-start(bf16[4,80,256]{2,1,0:T(8,128)(2,1)S(1)} %pad_maximum_fusion.q_ref), channel_id=1, source_target_pairs={{0,96},{1,97},{2,98},{3,99},{4,28},{5,29},{6,30},{7,31},{8,104},{9... | collective-permute-start | bytes 491528 | tf_op jit(solution)/shard_map/ppermute | solution.py:52
  72.5 15.0 %collective-permute-start.12 = (f32[4,136,256]{2,1,0:T(8,128)S(1)}, f32[4,136,256]{2,1,0:T(8,128)S(1)}, u32[]{:S(2)}, u32[]{:S(2)}) collective-permute-start(f32[4,136,256]{2,1,0:T(8,128)S(1)} %attend.6), channel_id=1, source_target_pairs={{0,64},{1,65},{2,66},{3,67},{4,20},{5,21},{6,22},{7,23},{8,72},{9,... | collective-permute-start | bytes 1671176 | tf_op jit(solution)/shard_map/ppermute | solution.py:52
  74.8 18.6 %collective-permute-start.11 = (f32[4,136,256]{2,1,0:T(8,128)S(1)}, f32[4,136,256]{2,1,0:T(8,128)S(1)}, u32[]{:S(2)}, u32[]{:S(2)}) collective-permute-start(f32[4,136,256]{2,1,0:T(8,128)S(1)} %attend.5), channel_id=1, source_target_pairs={{0,32},{1,33},{2,34},{3,35},{4,12},{5,13},{6,14},{7,15},{8,40},{9,... | collective-permute-start | bytes 1671176 | tf_op jit(solution)/shard_map/ppermute | solution.py:52
  75.1 18.3 %collective-permute-start.10 = (f32[4,136,256]{2,1,0:T(8,128)S(1)}, f32[4,136,256]{2,1,0:T(8,128)S(1)}, u32[]{:S(2)}, u32[]{:S(2)}) collective-permute-start(f32[4,136,256]{2,1,0:T(8,128)S(1)} %attend.4), channel_id=1, source_target_pairs={{0,96},{1,97},{2,98},{3,99},{4,28},{5,29},{6,30},{7,31},{8,104},{9... | collective-permute-start | bytes 1671176 | tf_op jit(solution)/shard_map/ppermute | solution.py:52
  93.6 0.7 copy-start.1
  94.3 3.9 %collective-permute-start.13 = (f32[136,256]{1,0:T(8,128)S(1)}, f32[136,256]{1,0:T(8,128)S(1)}, u32[]{:S(2)}, u32[]{:S(2)}) collective-permute-start(f32[136,256]{1,0:T(8,128)S(1)} %get-tuple-element.34), channel_id=1, source_target_pairs={{0,24},{1,25},{2,26},{3,27},{4,100},{5,101},{6,102},{7,103},{8,0},... | collective-permute-start | bytes 417800 | tf_op jit(solution)/shard_map/ppermute | solution.py:52
  95.4 6.9 %collective-permute-start.14 = (f32[136,256]{1,0:T(8,128)S(1)}, f32[136,256]{1,0:T(8,128)S(1)}, u32[]{:S(2)}, u32[]{:S(2)}) collective-permute-start(f32[136,256]{1,0:T(8,128)S(1)} %get-tuple-element.35), channel_id=1, source_target_pairs={{0,8},{1,9},{2,10},{3,11},{4,36},{5,37},{6,38},{7,39},{8,16},{9,17... | collective-permute-start | bytes 417800 | tf_op jit(solution)/shard_map/ppermute | solution.py:52
  95.8 6.6 %collective-permute-start.15 = (f32[136,256]{1,0:T(8,128)S(1)}, f32[136,256]{1,0:T(8,128)S(1)}, u32[]{:S(2)}, u32[]{:S(2)}) collective-permute-start(f32[136,256]{1,0:T(8,128)S(1)} %get-tuple-element.36), channel_id=1, source_target_pairs={{0,16},{1,17},{2,18},{3,19},{4,68},{5,69},{6,70},{7,71},{8,24},{9,... | collective-permute-start | bytes 417800 | tf_op jit(solution)/shard_map/ppermute | solution.py:52
  98.2 4.2 %copy-start.7 = (f32[136,256]{1,0:T(8,128)}, f32[136,256]{1,0:T(8,128)S(1)}, u32[]{:S(2)}) copy-start(f32[136,256]{1,0:T(8,128)S(1)} %collective-permute-done.13.b_ref) | copy-start | bytes 417796
  102.3 0.7 copy-start.8
  102.3 0.7 copy-start.9
Sparse Core Ops, SparseCore 0:
  35.3 56.3 all-gather.1
